TPU v7x, 32 devices: a whole 2x2x4 slice. The times are simulated.
32 devices in a mesh: section: 2 (over y), ctx: 4 (over z), head: 4 (over x, core).
Axes of the slice: x: 2, y: 2, z: 4, core: 2. Of those that a mesh axis runs over, the one named last changes fastest.
Arguments:
- query: bfloat16 [2, 2048, 8192], P('section', 'ctx', 'head'), may hold values from -30 to 30
- keys: bfloat16 [2, 2048, 1024], P('section', 'ctx', 'head'), may hold values from -6 to 6
- values: bfloat16 [2, 2048, 1024], P('section', 'ctx', 'head'), may hold values from -6 to 6
- attended: bfloat16 [2, 2048, 8192], P('section', 'ctx', 'head'), may hold values from -2 to 2
- output_gradient: bfloat16 [2, 2048, 8192], P('section', 'ctx', 'head'), may hold values from -12 to 12
- segments: int32 [2, 2048], P('section', 'ctx'), may hold values from 0 to 2, as said below
Outputs:
- received_query: float32 [2, 2048, 8192], P('section', 'ctx', 'head')
- received_key: float32 [2, 2048, 1024], P('section', 'ctx', 'head')
- received_value: float32 [2, 2048, 1024], P('section', 'ctx', 'head')
Inputs may be any that keep to these rules, and one draw needn't show every extreme that they name: `segments`: document ids never fall with increasing position pos, and every document starts at a position that is a multiple of 64.
All inputs are finite; a program needn't handle non-finite values.
Results may differ from a plain program's by a relative error of at most 0.0057.
Values may be sent and summed in bfloat16 or wider, within the bound.
A program may use at most 128 MiB of HBM per device.

v0:
```python
import functools
import math

import jax
import jax.numpy as jnp
import numpy as np
from jax import lax
from jax.experimental import pallas as pl
from jax.experimental.pallas import tpu as pltpu
from jax.sharding import PartitionSpec as P

HEAD = 128
REP = 8
LOG2E = 1.4426950408889634
SCALE = 1.0 / math.sqrt(HEAD)
NEG = -1e30
NT = (((1,), (1,)), ((), ()))
NN = (((1,), (0,)), ((), ()))


def dot(a, b, dims=NN):
    return lax.dot_general(a, b, dims, preferred_element_type=jnp.float32)


def tables():
    idx = np.arange(HEAD)
    parity = np.zeros((HEAD, HEAD), np.int64)
    for level in range(HEAD.bit_length() - 1):
        bit = (idx >> level) & 1
        parity += bit[:, None] * bit[None, :]
    hadamard = np.where(parity % 2 == 0, 1.0, -1.0)
    signs = np.where((idx * 73 + 41) % 128 < 64, 1.0, -1.0)
    return (
        jnp.asarray(hadamard, jnp.bfloat16),
        jnp.asarray(signs[None, :], jnp.float32),
    )


def grads_kernel(
    count, half,
    info, q_ref, g_ref, a_ref, k_ref, v_ref, segq_ref, segk_ref, had_ref, sign_ref,
    out_ref, dkv_ref,
    s_ref, dk_acc, dv_acc, dq_acc, m_ref, l_ref, delta_ref,
):
    slab = 2 * half
    dk_acc[...] = jnp.zeros_like(dk_acc)
    dv_acc[...] = jnp.zeros_like(dv_acc)

    def key_row(j):
        row = jnp.where(j < count, j * slab, (2 * count - 1 - j) * slab + half)
        return pl.multiple_of(row, half)

    def do_half(h, _):
        block = info[h]
        start = info[2 + h]
        rows = pl.ds(pl.multiple_of(h * half, half), half)
        segq = segq_ref[h]
        qpos = block * half + lax.broadcasted_iota(jnp.int32, (1, half), 1)
        m_ref[...] = jnp.full_like(m_ref, NEG)
        l_ref[...] = jnp.zeros_like(l_ref)
        dq_acc[...] = jnp.zeros_like(dq_acc)
        for r in range(REP):
            cols = slice(r * HEAD, (r + 1) * HEAD)
            prod = g_ref[rows, cols].astype(jnp.float32) * a_ref[rows, cols].astype(jnp.float32)
            delta_ref[r] = jnp.sum(prod.T, axis=0, keepdims=True)

        def first(j, _):
            row = pl.ds(key_row(j), half)
            at = pl.ds(pl.multiple_of(j * half, half), half)
            kj = k_ref[row, :]
            kpos = j * half + lax.broadcasted_iota(jnp.int32, (half, 1), 0)
            seen = (kpos <= qpos) & (segk_ref[row, :] == segq)
            bias = jnp.where(seen, 0.0, NEG)
            for r in range(REP):
                qr = q_ref[rows, r * HEAD:(r + 1) * HEAD]
                t = dot(kj, qr, NT) * (SCALE * LOG2E) + bias
                s_ref[r, at, :] = t
                t = t.reshape(half // 8, 8, half)
                m = m_ref[r]
                new = jnp.maximum(m, jnp.max(t, axis=0))
                m_ref[r] = new
                l_ref[r] = l_ref[r] * jnp.exp2(m - new) + jnp.sum(
                    jnp.exp2(t - new[None]), axis=0
                )
            return 0

        lax.fori_loop(start, block + 1, first, 0)
        for r in range(REP):
            m = m_ref[r]
            top = jnp.max(m, axis=0, keepdims=True)
            total = jnp.sum(l_ref[r] * jnp.exp2(m - top), axis=0, keepdims=True)
            m_ref[r, 0:1, :] = top + jnp.log(total) * LOG2E

        def second(j, _):
            row = pl.ds(key_row(j), half)
            at = pl.ds(pl.multiple_of(j * half, half), half)
            kt = k_ref[row, :].astype(jnp.float32).T.astype(jnp.bfloat16)
            vj = v_ref[row, :]
            dk = dk_acc[row, :]
            dv = dv_acc[row, :]
            for r in range(REP):
                cols = slice(r * HEAD, (r + 1) * HEAD)
                qr = q_ref[rows, cols]
                gr = g_ref[rows, cols]
                p = jnp.exp2(s_ref[r, at, :] - m_ref[r, 0:1, :])
                dp = dot(vj, gr, NT)
                ds = (p * (dp - delta_ref[r])).astype(jnp.bfloat16)
                dv = dv + dot(p.astype(jnp.bfloat16), gr)
                dk = dk + dot(ds, qr)
                dq_acc[r] += dot(kt, ds)
            dk_acc[row, :] = dk
            dv_acc[row, :] = dv
            return 0

        lax.fori_loop(start, block + 1, second, 0)
        for r in range(REP):
            dq = dq_acc[r].T * SCALE * sign_ref[...]
            turned = dot(dq.astype(jnp.bfloat16), had_ref[...]) * SCALE
            out_ref[rows, r * HEAD:(r + 1) * HEAD] = turned.astype(jnp.bfloat16)
        return 0

    lax.fori_loop(0, 2, do_half, 0)
    dkv_ref[:, :HEAD] = (dk_acc[...] * SCALE).astype(jnp.bfloat16)
    dkv_ref[:, HEAD:] = dv_acc[...].astype(jnp.bfloat16)


def group_grads(group, count, info, query, grad, att, kv, segq, segk, had, signs):
    tok = query.shape[0]
    half = tok // 2
    total = kv.shape[0]
    wide = REP * HEAD
    whole = lambda i, s: (0, 0)
    mine = lambda i, s: (0, group)
    return pl.pallas_call(
        functools.partial(grads_kernel, count, half),
        out_shape=(
            jax.ShapeDtypeStruct((tok, wide), jnp.bfloat16),
            jax.ShapeDtypeStruct((total, 2 * HEAD), jnp.bfloat16),
        ),
        grid_spec=pltpu.PrefetchScalarGridSpec(
            num_scalar_prefetch=1,
            grid=(1,),
            in_specs=[
                pl.BlockSpec((tok, wide), mine),
                pl.BlockSpec((tok, wide), mine),
                pl.BlockSpec((tok, wide), mine),
                pl.BlockSpec((total, HEAD), lambda i, s: (0, 0)),
                pl.BlockSpec((total, HEAD), lambda i, s: (0, 1)),
                pl.BlockSpec((2, 1, half), lambda i, s: (0, 0, 0)),
                pl.BlockSpec((total, 1), whole),
                pl.BlockSpec((HEAD, HEAD), whole),
                pl.BlockSpec((1, HEAD), whole),
            ],
            out_specs=(
                pl.BlockSpec((tok, wide), whole),
                pl.BlockSpec((total, 2 * HEAD), whole),
            ),
            scratch_shapes=[
                pltpu.VMEM((REP, total, half), jnp.float32),
                pltpu.VMEM((total, HEAD), jnp.float32),
                pltpu.VMEM((total, HEAD), jnp.float32),
                pltpu.VMEM((REP, HEAD, half), jnp.float32),
                pltpu.VMEM((REP, 8, half), jnp.float32),
                pltpu.VMEM((REP, 8, half), jnp.float32),
                pltpu.VMEM((REP, 1, half), jnp.float32),
            ],
        ),
        compiler_params=pltpu.CompilerParams(vmem_limit_bytes=56 * 1024 * 1024),
        cost_estimate=pl.CostEstimate(
            flops=12 * 10**9, bytes_accessed=8 * 10**6, transcendentals=9 * 10**6
        ),
        name="group_grads",
    )(info, query, grad, att, kv, kv, segq, segk, had, signs)


def pack_kernel(parts, *refs):
    had_ref, sign_ref, out_ref = refs[parts:]
    total = refs[0][...].astype(jnp.float32)
    for part in refs[1:parts]:
        total = total + part[...].astype(jnp.float32)
    for c in range(out_ref.shape[1] // HEAD):
        cols = slice(c * HEAD, (c + 1) * HEAD)
        flipped = (total[:, cols] * sign_ref[...]).astype(jnp.bfloat16)
        out_ref[:, cols] = (dot(flipped, had_ref[...]) * SCALE).astype(jnp.bfloat16)


def pack_sum(parts, had, signs):
    return pl.pallas_call(
        functools.partial(pack_kernel, len(parts)),
        out_shape=jax.ShapeDtypeStruct(parts[0].shape, jnp.bfloat16),
        name="pack_sum",
    )(*parts, had, signs)


def unpack_kernel(x_ref, had_ref, sign_ref, *rest):
    out_ref = rest[-1]
    for c in range(out_ref.shape[1] // HEAD):
        cols = slice(c * HEAD, (c + 1) * HEAD)
        out_ref[:, cols] = dot(x_ref[:, cols], had_ref[...]) * SCALE * sign_ref[...]


def unpack_query(packed, group, columns, held, had, signs):
    tok, wide = packed.shape
    part = tok // 2
    specs = [
        pl.BlockSpec((part, wide), lambda i: (i, 0)),
        pl.BlockSpec((HEAD, HEAD), lambda i: (0, 0)),
        pl.BlockSpec((1, HEAD), lambda i: (0, 0)),
    ]
    args = (packed, had, signs)
    alias = {}
    if held is not None:
        specs.append(pl.BlockSpec(memory_space=pl.ANY))
        args = args + (held,)
        alias = {3: 0}
    return pl.pallas_call(
        unpack_kernel,
        out_shape=jax.ShapeDtypeStruct((tok, columns), jnp.float32),
        grid=(2,),
        in_specs=specs,
        out_specs=pl.BlockSpec((part, wide), lambda i: (i, group)),
        input_output_aliases=alias,
        compiler_params=pltpu.CompilerParams(vmem_limit_bytes=32 * 1024 * 1024),
        name="unpack_query",
    )(*args)


def unpack_kv_kernel(groups, *refs):
    had_ref, sign_ref, key_ref, value_ref = refs[groups:]
    for g in range(groups):
        cols = slice(g * HEAD, (g + 1) * HEAD)
        for i, out in enumerate((key_ref, value_ref)):
            part = refs[g][:, i * HEAD:(i + 1) * HEAD]
            out[:, cols] = dot(part, had_ref[...]) * SCALE * sign_ref[...]


def unpack_kv(packed, had, signs):
    tok = packed[0].shape[0]
    shape = jax.ShapeDtypeStruct((tok, len(packed) * HEAD), jnp.float32)
    return pl.pallas_call(
        functools.partial(unpack_kv_kernel, len(packed)),
        out_shape=(shape, shape),
        name="unpack_kv",
    )(*packed, had, signs)


def shift(value, axis, steps):
    count = lax.axis_size(axis)
    pairs = [(source, (source + steps) % count) for source in range(count)]
    return lax.ppermute(value, axis, pairs)


def on_device(query, keys, values, attended, output_gradient, segments):
    query, keys, values = query[0], keys[0], values[0]
    attended, grad, seg = attended[0], output_gradient[0], segments[0]
    tok, columns = query.shape
    half = tok // 2
    groups = keys.shape[1] // HEAD
    count = lax.axis_size("ctx")
    me = lax.axis_index("ctx")
    had, signs = tables()

    seg_all = lax.all_gather(seg, "ctx", axis=0, tiled=True)
    by_half = seg_all.reshape(count, 2, half)
    last = jnp.concatenate([by_half[:, 0, -1], by_half[::-1, 1, -1]])
    starts = [jnp.sum((last < seg[h * half]).astype(jnp.int32)) for h in range(2)]
    info = jnp.stack([me, 2 * count - 1 - me] + starts).astype(jnp.int32)
    segq = seg.reshape(2, 1, half)
    segk = seg_all.reshape(count * tok, 1)

    gathered = []
    for g in range(groups):
        cols = slice(g * HEAD, (g + 1) * HEAD)
        kv = jnp.concatenate([keys[:, cols], values[:, cols]], axis=1)
        if g == 0:
            gathered.append(lax.all_gather(kv, "ctx", axis=0, tiled=True))
        else:
            pieces = [kv] + [shift(kv, "ctx", k) for k in range(1, count)]
            whole = jnp.zeros((count * tok, 2 * HEAD), kv.dtype)
            for k, piece in enumerate(pieces):
                at = (me - k) % count * tok
                whole = lax.dynamic_update_slice(whole, piece, (at, 0))
            gathered.append(whole)

    received, packed_kv = [], []
    for g in range(groups):
        packed, dkv = group_grads(
            g, count, info, query, grad, attended, gathered[g], segq, segk, had, signs
        )
        received.append(shift(packed, "section", -1))
        parts = []
        for k in range(count):
            part = lax.dynamic_slice(dkv, ((me + k) % count * tok, 0), (tok, 2 * HEAD))
            parts.append(part if k == 0 else shift(part, "ctx", k))
        packed_kv.append(shift(pack_sum(parts, had, signs), "section", -1))

    out = None
    for g in range(groups):
        out = unpack_query(received[g], g, columns, out, had, signs)
    out_key, out_value = unpack_kv(packed_kv, had, signs)
    return (out[None], out_key[None], out_value[None])


def solution(mesh):
    spec = P("section", "ctx", "head")
    return jax.shard_map(
        on_device,
        mesh=mesh,
        in_specs=(spec, spec, spec, spec, spec, P("section", "ctx")),
        out_specs=(spec, spec, spec),
        check_vma=False,
    )
```

profile of v0, /device:TPU:26, one launch (start us, length us, event | category | flops | bytes accessed | tf_op | source)
XLA Modules:
  0.0 197.6 jit_solution(2678227302432412869)
XLA Ops:
  7.2 1.1 fusion.2
  8.9 2.5 %collective-permute-start = (bf16[512,256]{1,0:T(8,128)(2,1)S(1)}, bf16[512,256]{1,0:T(8,128)(2,1)S(1)}, u32[]{:S(2)}, u32[]{:S(2)}) collective-permute-start(bf16[512,256]{1,0:T(8,128)(2,1)S(1)} %get-tuple-element.29), channel_id=1, source_target_pairs={{0,4},{4,8},{8,12},{12,0},{1,5},{5,9},{9,13},{13,1},{2,6},{6,10},{... | collective-permute-start | bytes 786440 | tf_op jit(solution)/shard_map/ppermute | solution.py:250
  11.4 0.7 pad_maximum_fusion.1
  12.2 40.9 %all-gather = s32[1,2048]{1,0:T(1,128)S(1)} all-gather(s32[1,512]{1,0:T(1,128)S(1)} %copy-done.11), channel_id=2, replica_groups=mesh['section'=2,'ctx'=4,'head'=4] {'ctx'}, dimensions={1}, use_global_device_ids=true | all-gather | bytes 10240 | tf_op jit(solution)/shard_map/all_gather | solution.py:263
  55.2 2.0 %fusion = (s32[]{:T(128)}, s32[]{:T(128)}) fusion(s32[]{:T(128)} %bitcast.4, s32[4]{0:T(128)S(1)} %bitcast.25, s32[4]{0:T(128)S(1)} %bitcast.24, s32[]{:T(128)} %bitcast.6), kind=kLoop, calls=%fused_computation.16 | loop fusion | flops 54 | bytes 48 | tf_op jit(solution)/shard_map/reduce_sum | solution.py:266
  57.2 1.8 pad_add_fusion.1.info
  59.0 1.4 copy.16.segk_ref
  60.5 1.0 copy-done.3
  61.5 31.1 %group_grads.2 = (bf16[512,1024]{1,0:T(8,128)(2,1)}, bf16[2048,256]{1,0:T(8,128)(2,1)}) custom-call(s32[4]{0:T(128)} %pad_add_fusion.1.info, bf16[512,2048]{1,0:T(8,128)(2,1)} %bitcast.26, bf16[512,2048]{1,0:T(8,128)(2,1)} %bitcast.28, bf16[512,2048]{1,0:T(8,128)(2,1)} %bitcast.30, bf16[2048,256]{1,0:T(8,128)(2,1)} %copy-done.3, ...), custom_call_target="tpu_custom_call" | custom-call | flops 12000000000 | bytes 8000000 | tf_op jit(solution)/shard_map/group_grads/pallas_call | solution.py:134
  92.6 31.1 %group_grads.3 = (bf16[512,1024]{1,0:T(8,128)(2,1)}, bf16[2048,256]{1,0:T(8,128)(2,1)}) custom-call(s32[4]{0:T(128)} %pad_add_fusion.1.info, bf16[512,2048]{1,0:T(8,128)(2,1)} %bitcast.27, bf16[512,2048]{1,0:T(8,128)(2,1)} %bitcast.29, bf16[512,2048]{1,0:T(8,128)(2,1)} %bitcast.31, bf16[2048,256]{1,0:T(8,128)(2,1)} %all-gather.3.cloned.1.call-done.k_ref.v_ref, ...), custom_call_target="tpu_custom_call" | custom-call | flops 12000000000 | bytes 8000000 | tf_op jit(solution)/shard_map/group_grads/pallas_call | solution.py:134
  123.8 2.0 %collective-permute-start.3 = (bf16[512,1024]{1,0:T(8,128)(2,1)}, bf16[512,1024]{1,0:T(8,128)(2,1)S(1)}, u32[]{:S(2)}, u32[]{:S(2)}) collective-permute-start(bf16[512,1024]{1,0:T(8,128)(2,1)} %get-tuple-element.9), channel_id=1, source_target_pairs={{0,16},{16,0},{1,17},{17,1},{2,18},{18,2},{3,19},{19,3},{4,20},{20... | collective-permute-start | bytes 3145736 | tf_op jit(solution)/shard_map/ppermute | solution.py:250
  125.8 2.0 %constant_dynamic-slice_fusion = (bf16[512,256]{1,0:T(8,128)(2,1)S(1)}, bf16[512,256]{1,0:T(8,128)(2,1)S(1)}, bf16[512,256]{1,0:T(8,128)(2,1)S(1)}, bf16[512,256]{1,0:T(8,128)(2,1)}) fusion(bf16[2048,256]{1,0:T(8,128)(2,1)} %get-tuple-element.12, s32[]{:T(128)S(6)} %select_n.80, s32[]{:T(128)S(6)} %select_n.78, s32[]{:T(128)S(6)} %select_n.76, s32[]{:T(128)S(6)} %select_n.68), kind=kLoop, calls=%fused_computation.2 | loop fusion | bytes 2097168 | tf_op jit(solution)/shard_map/dynamic_slice | solution.py:293
  127.8 3.8 %collective-permute-start.9 = (bf16[512,256]{1,0:T(8,128)(2,1)S(1)}, bf16[512,256]{1,0:T(8,128)(2,1)S(1)}, u32[]{:S(2)}, u32[]{:S(2)}) collective-permute-start(bf16[512,256]{1,0:T(8,128)(2,1)S(1)} %get-tuple-element.19), channel_id=1, source_target_pairs={{0,4},{4,8},{8,12},{12,0},{1,5},{5,9},{9,13},{13,1},{2,6},{6,10},{... | collective-permute-start | bytes 786440 | tf_op jit(solution)/shard_map/ppermute | solution.py:250
  131.6 0.9 constant_dynamic-slice_fusion.4
  132.5 6.4 %collective-permute-done.11.refs_3_ = bf16[512,256]{1,0:T(8,128)(2,1)S(1)} collective-permute-done((bf16[512,256]{1,0:T(8,128)(2,1)S(1)}, bf16[512,256]{1,0:T(8,128)(2,1)S(1)}, u32[]{:S(2)}, u32[]{:S(2)}) %collective-permute-start.11) | collective-permute-done | bytes 262176 | tf_op jit(solution)/shard_map/ppermute | solution.py:250
  138.9 19.1 %collective-permute-done.10.refs_2_ = bf16[512,256]{1,0:T(8,128)(2,1)S(1)} collective-permute-done((bf16[512,256]{1,0:T(8,128)(2,1)S(1)}, bf16[512,256]{1,0:T(8,128)(2,1)S(1)}, u32[]{:S(2)}, u32[]{:S(2)}) %collective-permute-start.10) | collective-permute-done | bytes 262176 | tf_op jit(solution)/shard_map/ppermute | solution.py:250
  158.8 2.2 %pack_sum.3 = bf16[512,256]{1,0:T(8,128)(2,1)} custom-call(bf16[512,256]{1,0:T(8,128)(2,1)} %get-tuple-element.20.refs_0_, bf16[512,256]{1,0:T(8,128)(2,1)} %copy-done.7, bf16[512,256]{1,0:T(8,128)(2,1)} %copy-done.5, bf16[512,256]{1,0:T(8,128)(2,1)} %copy-done.4, bf16[128,128]{1,0:T(8,128)(2,1)} %constant.76.clone.had_ref.refs_4_.refs_2_, ...), custom_call_target="tpu_custom_call" | custom-call | tf_op jit(solution)/shard_map/pack_sum/pallas_call | solution.py:188
  161.3 8.0 %collective-permute-done.6.refs_2_ = bf16[512,256]{1,0:T(8,128)(2,1)S(1)} collective-permute-done((bf16[512,256]{1,0:T(8,128)(2,1)}, bf16[512,256]{1,0:T(8,128)(2,1)S(1)}, u32[]{:S(2)}, u32[]{:S(2)}) %collective-permute-start.6) | collective-permute-done | bytes 262176 | tf_op jit(solution)/shard_map/ppermute | solution.py:250
  169.3 4.2 %collective-permute-done.5.refs_1_ = bf16[512,256]{1,0:T(8,128)(2,1)S(1)} collective-permute-done((bf16[512,256]{1,0:T(8,128)(2,1)S(1)}, bf16[512,256]{1,0:T(8,128)(2,1)S(1)}, u32[]{:S(2)}, u32[]{:S(2)}) %collective-permute-start.5) | collective-permute-done | bytes 262176 | tf_op jit(solution)/shard_map/ppermute | solution.py:250
  174.2 2.2 %pack_sum.2 = bf16[512,256]{1,0:T(8,128)(2,1)} custom-call(bf16[512,256]{1,0:T(8,128)(2,1)} %get-tuple-element.24.refs_0_, bf16[512,256]{1,0:T(8,128)(2,1)} %copy-done.9, bf16[512,256]{1,0:T(8,128)(2,1)} %copy-done.8, bf16[512,256]{1,0:T(8,128)(2,1)} %copy-done.6, bf16[128,128]{1,0:T(8,128)(2,1)} %constant.76.clone.had_ref.refs_4_.refs_2_, ...), custom_call_target="tpu_custom_call" | custom-call | tf_op jit(solution)/shard_map/pack_sum/pallas_call | solution.py:188
  176.7 7.9 %collective-permute-done.8.refs_0_ = bf16[512,256]{1,0:T(8,128)(2,1)S(1)} collective-permute-done((bf16[512,256]{1,0:T(8,128)(2,1)}, bf16[512,256]{1,0:T(8,128)(2,1)S(1)}, u32[]{:S(2)}, u32[]{:S(2)}) %collective-permute-start.8) | collective-permute-done | bytes 262176 | tf_op jit(solution)/shard_map/ppermute | solution.py:250
  185.2 2.3 %unpack_kv.1 = (f32[512,256]{1,0:T(8,128)}, f32[512,256]{1,0:T(8,128)}) custom-call(bf16[512,256]{1,0:T(8,128)(2,1)} %copy-done.10, bf16[512,256]{1,0:T(8,128)(2,1)} %collective-permute-done.12.refs_1_, bf16[128,128]{1,0:T(8,128)(2,1)} %constant.76.clone.had_ref.refs_4_.refs_2_, f32[1,128]{1,0:T(1,128)} %constant.77.clone.sign_ref.refs_5_.refs_3_), custom_call_target="tpu_custom_call" | custom-call | tf_op jit(solution)/shard_map/unpack_kv/pallas_call | solution.py:240
  187.5 1.6 unpack_query.2.rest_0_
  189.1 1.6 unpack_query.3
  (57 shorter events, 5.6 us)
Async XLA Ops:
  7.2 5.0 %copy-start.11 = (s32[1,512]{1,0:T(1,128)S(1)}, s32[1,512]{1,0:T(1,128)}, u32[]{:S(2)}) copy-start(s32[1,512]{1,0:T(1,128)} %param.13) | copy-start | bytes 6148
  7.2 85.4 %all-gather.3.cloned.1.call-start = ((), (), s32[]{:S(2)}) async-start(), calls=%async_computation | async-start | bytes 1310720 | tf_op jit(solution)/shard_map/all_gather | solution.py:276
  8.5 51.9 %collective-permute-start.1 = (bf16[512,256]{1,0:T(8,128)(2,1)S(1)}, bf16[512,256]{1,0:T(8,128)(2,1)S(1)}, u32[]{:S(2)}, u32[]{:S(2)}) collective-permute-start(bf16[512,256]{1,0:T(8,128)(2,1)S(1)} %get-tuple-element.29), channel_id=1, source_target_pairs={{0,8},{4,12},{8,0},{12,4},{1,9},{5,13},{9,1},{13,5},{2,10},{6,14},... | collective-permute-start | bytes 786440 | tf_op jit(solution)/shard_map/ppermute | solution.py:250
  8.9 51.5 %collective-permute-start = (bf16[512,256]{1,0:T(8,128)(2,1)S(1)}, bf16[512,256]{1,0:T(8,128)(2,1)S(1)}, u32[]{:S(2)}, u32[]{:S(2)}) collective-permute-start(bf16[512,256]{1,0:T(8,128)(2,1)S(1)} %get-tuple-element.29), channel_id=1, source_target_pairs={{0,4},{4,8},{8,12},{12,0},{1,5},{5,9},{9,13},{13,1},{2,6},{6,10},{... | collective-permute-start | bytes 786440 | tf_op jit(solution)/shard_map/ppermute | solution.py:250
  11.4 49.1 %collective-permute-start.2 = (bf16[512,256]{1,0:T(8,128)(2,1)S(1)}, bf16[512,256]{1,0:T(8,128)(2,1)S(1)}, u32[]{:S(2)}, u32[]{:S(2)}) collective-permute-start(bf16[512,256]{1,0:T(8,128)(2,1)S(1)} %get-tuple-element.29), channel_id=1, source_target_pairs={{0,12},{4,0},{8,4},{12,8},{1,13},{5,1},{9,5},{13,9},{2,14},{6,2},{... | collective-permute-start | bytes 786440 | tf_op jit(solution)/shard_map/ppermute | solution.py:250
  60.5 1.0 copy-start.3
  123.8 7.8 %copy-start.2 = (bf16[2048,256]{1,0:T(8,128)(2,1)S(1)}, bf16[2048,256]{1,0:T(8,128)(2,1)}, u32[]{:S(2)}) copy-start(bf16[2048,256]{1,0:T(8,128)(2,1)} %get-tuple-element.11) | copy-start | bytes 3145732
  123.8 63.8 %collective-permute-start.4 = (bf16[512,1024]{1,0:T(8,128)(2,1)}, bf16[512,1024]{1,0:T(8,128)(2,1)S(1)}, u32[]{:S(2)}, u32[]{:S(2)}) collective-permute-start(bf16[512,1024]{1,0:T(8,128)(2,1)} %get-tuple-element.10), channel_id=1, source_target_pairs={{0,16},{16,0},{1,17},{17,1},{2,18},{18,2},{3,19},{19,3},{4,20},{20... | collective-permute-start | bytes 3145736 | tf_op jit(solution)/shard_map/ppermute | solution.py:250
  123.8 65.4 %collective-permute-start.3 = (bf16[512,1024]{1,0:T(8,128)(2,1)}, bf16[512,1024]{1,0:T(8,128)(2,1)S(1)}, u32[]{:S(2)}, u32[]{:S(2)}) collective-permute-start(bf16[512,1024]{1,0:T(8,128)(2,1)} %get-tuple-element.9), channel_id=1, source_target_pairs={{0,16},{16,0},{1,17},{17,1},{2,18},{18,2},{3,19},{19,3},{4,20},{20... | collective-permute-start | bytes 3145736 | tf_op jit(solution)/shard_map/ppermute | solution.py:250
  127.8 11.1 %collective-permute-start.11 = (bf16[512,256]{1,0:T(8,128)(2,1)S(1)}, bf16[512,256]{1,0:T(8,128)(2,1)S(1)}, u32[]{:S(2)}, u32[]{:S(2)}) collective-permute-start(bf16[512,256]{1,0:T(8,128)(2,1)S(1)} %get-tuple-element.17), channel_id=1, source_target_pairs={{0,12},{4,0},{8,4},{12,8},{1,13},{5,1},{9,5},{13,9},{2,14},{6,2},{... | collective-permute-start | bytes 786440 | tf_op jit(solution)/shard_map/ppermute | solution.py:250
  127.8 30.2 %collective-permute-start.10 = (bf16[512,256]{1,0:T(8,128)(2,1)S(1)}, bf16[512,256]{1,0:T(8,128)(2,1)S(1)}, u32[]{:S(2)}, u32[]{:S(2)}) collective-permute-start(bf16[512,256]{1,0:T(8,128)(2,1)S(1)} %get-tuple-element.18), channel_id=1, source_target_pairs={{0,8},{4,12},{8,0},{12,4},{1,9},{5,13},{9,1},{13,5},{2,10},{6,14},... | collective-permute-start | bytes 786440 | tf_op jit(solution)/shard_map/ppermute | solution.py:250
  127.8 30.2 %collective-permute-start.9 = (bf16[512,256]{1,0:T(8,128)(2,1)S(1)}, bf16[512,256]{1,0:T(8,128)(2,1)S(1)}, u32[]{:S(2)}, u32[]{:S(2)}) collective-permute-start(bf16[512,256]{1,0:T(8,128)(2,1)S(1)} %get-tuple-element.19), channel_id=1, source_target_pairs={{0,4},{4,8},{8,12},{12,0},{1,5},{5,9},{9,13},{13,1},{2,6},{6,10},{... | collective-permute-start | bytes 786440 | tf_op jit(solution)/shard_map/ppermute | solution.py:250
  132.5 55.0 %copy-start = (bf16[128,128]{1,0:T(8,128)(2,1)S(1)}, bf16[128,128]{1,0:T(8,128)(2,1)}, u32[]{:S(2)}) copy-start(bf16[128,128]{1,0:T(8,128)(2,1)} %constant.76.clone.had_ref.refs_4_.refs_2_) | copy-start | bytes 98308
  132.5 55.0 %copy-start.1 = (f32[1,128]{1,0:T(1,128)S(1)}, f32[1,128]{1,0:T(1,128)}, u32[]{:S(2)}) copy-start(f32[1,128]{1,0:T(1,128)} %constant.77.clone.sign_ref.refs_5_.refs_3_) | copy-start | bytes 1540
  138.9 19.2 %copy-start.4 = (bf16[512,256]{1,0:T(8,128)(2,1)}, bf16[512,256]{1,0:T(8,128)(2,1)S(1)}, u32[]{:S(2)}) copy-start(bf16[512,256]{1,0:T(8,128)(2,1)S(1)} %collective-permute-done.11.refs_3_) | copy-start | bytes 786436
  138.9 22.1 %collective-permute-start.7 = (bf16[512,256]{1,0:T(8,128)(2,1)}, bf16[512,256]{1,0:T(8,128)(2,1)S(1)}, u32[]{:S(2)}, u32[]{:S(2)}) collective-permute-start(bf16[512,256]{1,0:T(8,128)(2,1)} %get-tuple-element.21), channel_id=1, source_target_pairs={{0,12},{4,0},{8,4},{12,8},{1,13},{5,1},{9,5},{13,9},{2,14},{6,2},{... | collective-permute-start | bytes 786440 | tf_op jit(solution)/shard_map/ppermute | solution.py:250
  158.0 11.3 %collective-permute-start.6 = (bf16[512,256]{1,0:T(8,128)(2,1)}, bf16[512,256]{1,0:T(8,128)(2,1)S(1)}, u32[]{:S(2)}, u32[]{:S(2)}) collective-permute-start(bf16[512,256]{1,0:T(8,128)(2,1)} %get-tuple-element.22), channel_id=1, source_target_pairs={{0,8},{4,12},{8,0},{12,4},{1,9},{5,13},{9,1},{13,5},{2,10},{6,14},... | collective-permute-start | bytes 786440 | tf_op jit(solution)/shard_map/ppermute | solution.py:250
  158.0 0.8 copy-start.7
  158.0 15.5 %collective-permute-start.5 = (bf16[512,256]{1,0:T(8,128)(2,1)S(1)}, bf16[512,256]{1,0:T(8,128)(2,1)S(1)}, u32[]{:S(2)}, u32[]{:S(2)}) collective-permute-start(bf16[512,256]{1,0:T(8,128)(2,1)S(1)} %get-tuple-element.23), channel_id=1, source_target_pairs={{0,4},{4,8},{8,12},{12,0},{1,5},{5,9},{9,13},{13,1},{2,6},{6,10},{... | collective-permute-start | bytes 786440 | tf_op jit(solution)/shard_map/ppermute | solution.py:250
  161.0 12.5 %copy-start.6 = (bf16[512,256]{1,0:T(8,128)(2,1)}, bf16[512,256]{1,0:T(8,128)(2,1)S(1)}, u32[]{:S(2)}) copy-start(bf16[512,256]{1,0:T(8,128)(2,1)S(1)} %collective-permute-done.7.refs_3_) | copy-start | bytes 786436
  161.0 15.7 %collective-permute-start.12 = (bf16[512,256]{1,0:T(8,128)(2,1)}, bf16[512,256]{1,0:T(8,128)(2,1)}, u32[]{:S(2)}, u32[]{:S(2)}) collective-permute-start(bf16[512,256]{1,0:T(8,128)(2,1)} %pack_sum.3), channel_id=1, source_target_pairs={{0,16},{16,0},{1,17},{17,1},{2,18},{18,2},{3,19},{19,3},{4,20},{20... | collective-permute-start | bytes 786440 | tf_op jit(solution)/shard_map/ppermute | solution.py:250
  169.3 4.2 %copy-start.8 = (bf16[512,256]{1,0:T(8,128)(2,1)}, bf16[512,256]{1,0:T(8,128)(2,1)S(1)}, u32[]{:S(2)}) copy-start(bf16[512,256]{1,0:T(8,128)(2,1)S(1)} %collective-permute-done.6.refs_2_) | copy-start | bytes 786436
  173.5 0.7 copy-start.9
  176.3 8.2 %collective-permute-start.8 = (bf16[512,256]{1,0:T(8,128)(2,1)}, bf16[512,256]{1,0:T(8,128)(2,1)S(1)}, u32[]{:S(2)}, u32[]{:S(2)}) collective-permute-start(bf16[512,256]{1,0:T(8,128)(2,1)} %pack_sum.2), channel_id=1, source_target_pairs={{0,16},{16,0},{1,17},{17,1},{2,18},{18,2},{3,19},{19,3},{4,20},{20... | collective-permute-start | bytes 786440 | tf_op jit(solution)/shard_map/ppermute | solution.py:250
  (2 other events, 1.4 us)
Sparse Core Ops, SparseCore 0:
  12.3 39.3 all-gather.2
where the time goes:
time: 199 us; the launch traced here: 198 us
  Pallas kernels  72.1 us (36%)
  waiting for transfers between devices  45.6 us (23%)
  blocking collectives  40.9 us (21%)
  between operations  14.2 us (7%)
  local copies, waits for them, and re-layouts  10 us (5%)
  starting transfers between devices  9.44 us (5%)
  other arithmetic  5.31 us (3%)
    pallas_call x2, Pallas kernels, group_grads(): pl.pallas_call(functools.partial(grads_kernel, count, half), out_shape=(j...  62.3 us
    ppermute x13, waiting for transfers between devices, shift(): return lax.ppermute(value, axis, pairs)  45.6 us
    all_gather x1, blocking collectives, on_device(): seg_all = lax.all_gather(seg, 'ctx', axis=0, tiled=True)  40.9 us
    ppermute x13, starting transfers between devices, shift(): return lax.ppermute(value, axis, pairs)  9.41 us
    pallas_call x2, Pallas kernels, pack_sum(): pl.pallas_call(functools.partial(pack_kernel, len(parts)), out_shape=jax....  4.34 us
  transfers between devices with their start and end apart: 14, of which 5 were waited for; matrix products, arithmetic and copies ran while one was open for 6% of the time, Pallas kernels for 20%

commit v1 on v0

v1 whole, which is shorter than its diff:
```python
import functools
import math

import jax
import jax.numpy as jnp
import numpy as np
from jax import lax
from jax.experimental import pallas as pl
from jax.experimental.pallas import tpu as pltpu
from jax.sharding import PartitionSpec as P

HEAD = 128
REP = 8
LOG2E = 1.4426950408889634
SCALE = 1.0 / math.sqrt(HEAD)
NEG = -1e30
NT = (((1,), (1,)), ((), ()))
NN = (((1,), (0,)), ((), ()))


def dot(a, b, dims=NN):
    return lax.dot_general(a, b, dims, preferred_element_type=jnp.float32)


def tables():
    idx = np.arange(HEAD)
    parity = np.zeros((HEAD, HEAD), np.int64)
    for level in range(HEAD.bit_length() - 1):
        bit = (idx >> level) & 1
        parity += bit[:, None] * bit[None, :]
    hadamard = np.where(parity % 2 == 0, 1.0, -1.0)
    signs = np.where((idx * 73 + 41) % 128 < 64, 1.0, -1.0)
    return (
        jnp.asarray(hadamard, jnp.bfloat16),
        jnp.asarray(signs[None, :], jnp.float32),
    )


def mega_kernel(
    count, groups, half, sections,
    q_ref, g_ref, a_ref, k_ref, v_ref, seg_ref, had_ref, sign_ref,
    rq_ref, rkv_ref,
    kv_buf, seg_buf, dkv_out, part, own, q_pack, kv_pack,
    s_ref, dk_acc, dv_acc, dq_acc, m_ref, l_ref, delta_ref,
    kv_send, kv_recv, seg_send, seg_recv, part_send, part_recv,
    q_send, q_recv, back_send, back_recv,
):
    me = lax.axis_index("ctx")
    section = lax.axis_index("section")
    before = lax.rem(section + sections - 1, sections)
    after = lax.rem(section + 1, sections)
    wide = REP * HEAD

    def peer(d):
        return lax.rem(me + d, count)

    def remote(src, dst, send, recv, where):
        return pltpu.make_async_remote_copy(
            src_ref=src, dst_ref=dst, send_sem=send, recv_sem=recv,
            device_id=where, device_id_type=pl.DeviceIdType.MESH,
        )

    def kv_copy(g, h, slab, d, to):
        at = kv_buf.at[g, slab, h]
        return remote(at, at, kv_send.at[g, h, d], kv_recv.at[g, h, slab], {"ctx": to})

    def seg_copy(slab, d, to):
        at = seg_buf.at[slab]
        return remote(at, at, seg_send.at[d], seg_recv.at[slab], {"ctx": to})

    def part_copy(g, h, d, to):
        return remote(
            dkv_out.at[g, to, h], part.at[g, me, h],
            part_send.at[g, h, d], part_recv.at[g, h, me], {"ctx": to},
        )

    def part_arrival(g, h, source):
        at = part.at[g, source, h]
        return remote(at, at, part_send.at[g, h, 0], part_recv.at[g, h, source], {"ctx": source})

    def q_copy(g, h):
        return remote(
            q_pack.at[g, h], rq_ref.at[g, h], q_send.at[g, h], q_recv.at[g, h],
            {"section": before},
        )

    def back_copy(g):
        return remote(
            kv_pack.at[g], rkv_ref.at[g], back_send.at[g], back_recv.at[g],
            {"section": before},
        )

    barrier = pltpu.get_barrier_semaphore()
    for d in range(1, count):
        pl.semaphore_signal(
            barrier, inc=1, device_id={"ctx": peer(d)}, device_id_type=pl.DeviceIdType.MESH
        )
    pl.semaphore_signal(
        barrier, inc=1, device_id={"section": after}, device_id_type=pl.DeviceIdType.MESH
    )
    seg_buf[me] = seg_ref[...]
    for g in range(groups):
        for h in range(2):
            rows = slice(h * half, (h + 1) * half)
            cols = slice(g * HEAD, (g + 1) * HEAD)
            kv_buf[g, me, h, 0] = k_ref[rows, cols]
            kv_buf[g, me, h, 1] = v_ref[rows, cols]
    pl.semaphore_wait(barrier, count)

    for d in range(1, count):
        seg_copy(me, d, peer(d)).start()
    for g in range(groups):
        for d in range(1, count):
            kv_copy(g, 0, me, d, peer(d)).start()
        for d in range(1, count):
            @pl.when(peer(d) < me)
            def _():
                kv_copy(g, 1, me, d, peer(d)).start()

    for d in range(1, count):
        seg_copy(peer(d), d, peer(d)).wait_recv()

    def place(j):
        low = j < count
        return jnp.where(low, j, 2 * count - 1 - j), jnp.where(low, 0, 1)

    def do_group(g):
        base = g * wide
        dk_acc[...] = jnp.zeros_like(dk_acc)
        dv_acc[...] = jnp.zeros_like(dv_acc)

        def do_half(h, _):
            block = jnp.where(h == 0, me, 2 * count - 1 - me)
            rows = pl.ds(pl.multiple_of(h * half, half), half)
            segq = seg_ref[h, 0:1, :]
            qpos = block * half + lax.broadcasted_iota(jnp.int32, (1, half), 1)
            m_ref[...] = jnp.full_like(m_ref, NEG)
            l_ref[...] = jnp.zeros_like(l_ref)
            dq_acc[...] = jnp.zeros_like(dq_acc)
            for r in range(REP):
                cols = slice(base + r * HEAD, base + (r + 1) * HEAD)
                prod = g_ref[rows, cols].astype(jnp.float32) * a_ref[rows, cols].astype(
                    jnp.float32
                )
                delta_ref[r] = jnp.sum(prod.T, axis=0, keepdims=True)

            def first(j, _):
                slab, kh = place(j)
                fresh = jnp.where(h == 0, 0, me + 1)

                @pl.when((j >= fresh) & (j < block))
                def _():
                    kv_copy(g, kh, slab, 0, slab).wait_recv()

                at = pl.ds(pl.multiple_of(j * half, half), half)
                kj = kv_buf[g, slab, kh, 0]
                kpos = j * half + lax.broadcasted_iota(jnp.int32, (half, 1), 0)
                segrow = seg_buf[slab, kh, 0:1, :].astype(jnp.float32)
                segk = jnp.broadcast_to(segrow, (HEAD, half)).T[:, 0:1]
                seen = (kpos <= qpos) & (segk == segq.astype(jnp.float32))
                bias = jnp.where(seen, 0.0, NEG)
                for r in range(REP):
                    qr = q_ref[rows, base + r * HEAD:base + (r + 1) * HEAD]
                    t = dot(kj, qr, NT) * (SCALE * LOG2E) + bias
                    s_ref[r, at, :] = t
                    t = t.reshape(half // 8, 8, half)
                    m = m_ref[r]
                    new = jnp.maximum(m, jnp.max(t, axis=0))
                    m_ref[r] = new
                    l_ref[r] = l_ref[r] * jnp.exp2(m - new) + jnp.sum(
                        jnp.exp2(t - new[None]), axis=0
                    )
                return 0

            lax.fori_loop(0, block + 1, first, 0)
            for r in range(REP):
                m = m_ref[r]
                top = jnp.max(m, axis=0, keepdims=True)
                total = jnp.sum(l_ref[r] * jnp.exp2(m - top), axis=0, keepdims=True)
                m_ref[r, 0:1, :] = top + jnp.log(total) * LOG2E

            def second(j, _):
                slab, kh = place(j)
                at = pl.ds(pl.multiple_of(j * half, half), half)
                kt = kv_buf[g, slab, kh, 0].astype(jnp.float32).T.astype(jnp.bfloat16)
                vj = kv_buf[g, slab, kh, 1]
                dk = dk_acc[slab, kh]
                dv = dv_acc[slab, kh]
                for r in range(REP):
                    cols = slice(base + r * HEAD, base + (r + 1) * HEAD)
                    qr = q_ref[rows, cols]
                    gr = g_ref[rows, cols]
                    p = jnp.exp2(s_ref[r, at, :] - m_ref[r, 0:1, :])
                    dp = dot(vj, gr, NT)
                    ds = (p * (dp - delta_ref[r])).astype(jnp.bfloat16)
                    dv = dv + dot(p.astype(jnp.bfloat16), gr)
                    dk = dk + dot(ds, qr)
                    dq_acc[r] += dot(kt, ds)
                dk_acc[slab, kh] = dk
                dv_acc[slab, kh] = dv
                return 0

            lax.fori_loop(0, block + 1, second, 0)
            for r in range(REP):
                dq = dq_acc[r].T * SCALE * sign_ref[...]
                turned = dot(dq.astype(jnp.bfloat16), had_ref[...]) * SCALE
                q_pack[g, h, :, r * HEAD:(r + 1) * HEAD] = turned.astype(jnp.bfloat16)
            q_copy(g, h).start()
            return 0

        lax.fori_loop(0, 2, do_half, 0)
        for h in range(2):
            own[g, h, 0] = dk_acc[me, h] * SCALE
            own[g, h, 1] = dv_acc[me, h]
            for d in range(1, count):
                to = peer(d)

                def send():
                    dkv_out[g, to, h, 0] = (dk_acc[to, h] * SCALE).astype(jnp.bfloat16)
                    dkv_out[g, to, h, 1] = dv_acc[to, h].astype(jnp.bfloat16)
                    part_copy(g, h, d, to).start()

                if h == 0:
                    send()
                else:
                    pl.when(to > me)(send)

    def finish(g):
        for h in range(2):
            for d in range(1, count):
                source = peer(d)

                def add():
                    part_arrival(g, h, source).wait_recv()
                    own[g, h] += part[g, source, h].astype(jnp.float32)

                if h == 0:
                    add()
                else:
                    pl.when(source < me)(add)
            for i in range(2):
                flipped = (own[g, h, i] * sign_ref[...]).astype(jnp.bfloat16)
                kv_pack[g, h, i] = (dot(flipped, had_ref[...]) * SCALE).astype(jnp.bfloat16)
        back_copy(g).start()

    for g in range(groups):
        do_group(g)
    for g in range(groups):
        finish(g)

    for d in range(1, count):
        seg_copy(me, d, peer(d)).wait_send()
    for g in range(groups):
        for d in range(1, count):
            kv_copy(g, 0, me, d, peer(d)).wait_send()
            part_copy(g, 0, d, peer(d)).wait_send()

            @pl.when(peer(d) < me)
            def _():
                kv_copy(g, 1, me, d, peer(d)).wait_send()

            @pl.when(peer(d) > me)
            def _():
                part_copy(g, 1, d, peer(d)).wait_send()
        for h in range(2):
            q_copy(g, h).wait()
        back_copy(g).wait()


def exchange_grads(count, sections, query, grad, att, keys, values, seg, had, signs):
    tok, columns = query.shape
    half = tok // 2
    groups = keys.shape[1] // HEAD
    wide = REP * HEAD
    vmem = pl.BlockSpec(memory_space=pltpu.VMEM)
    anywhere = pl.BlockSpec(memory_space=pl.ANY)
    low, full = jnp.bfloat16, jnp.float32
    dma = pltpu.SemaphoreType.DMA
    return pl.pallas_call(
        functools.partial(mega_kernel, count, groups, half, sections),
        out_shape=(
            jax.ShapeDtypeStruct((groups, 2, half, wide), low),
            jax.ShapeDtypeStruct((groups, 2, 2, half, HEAD), low),
        ),
        in_specs=[vmem] * 8,
        out_specs=(anywhere, anywhere),
        scratch_shapes=[
            pltpu.VMEM((groups, count, 2, 2, half, HEAD), low),
            pltpu.VMEM((count, 2, 8, half), jnp.int32),
            pltpu.VMEM((groups, count, 2, 2, half, HEAD), low),
            pltpu.VMEM((groups, count, 2, 2, half, HEAD), low),
            pltpu.VMEM((groups, 2, 2, half, HEAD), full),
            pltpu.VMEM((groups, 2, half, wide), low),
            pltpu.VMEM((groups, 2, 2, half, HEAD), low),
            pltpu.VMEM((REP, count * tok, half), full),
            pltpu.VMEM((count, 2, half, HEAD), full),
            pltpu.VMEM((count, 2, half, HEAD), full),
            pltpu.VMEM((REP, HEAD, half), full),
            pltpu.VMEM((REP, 8, half), full),
            pltpu.VMEM((REP, 8, half), full),
            pltpu.VMEM((REP, 1, half), full),
            dma((groups, 2, count)),
            dma((groups, 2, count)),
            dma((count,)),
            dma((count,)),
            dma((groups, 2, count)),
            dma((groups, 2, count)),
            dma((groups, 2)),
            dma((groups, 2)),
            dma((groups,)),
            dma((groups,)),
        ],
        compiler_params=pltpu.CompilerParams(
            vmem_limit_bytes=60 * 1024 * 1024, collective_id=0, has_side_effects=True
        ),
        cost_estimate=pl.CostEstimate(
            flops=24 * 10**9, bytes_accessed=16 * 10**6, transcendentals=18 * 10**6
        ),
        name="exchange_grads",
    )(query, grad, att, keys, values, seg, had, signs)


def unpack_kernel(q_ref, kv_ref, had_ref, sign_ref, out_q, out_k, out_v):
    for c in range(REP):
        cols = slice(c * HEAD, (c + 1) * HEAD)
        out_q[:, cols] = dot(q_ref[0, 0, :, cols], had_ref[...]) * SCALE * sign_ref[...]
    out_k[...] = dot(kv_ref[0, 0, 0], had_ref[...]) * SCALE * sign_ref[...]
    out_v[...] = dot(kv_ref[0, 0, 1], had_ref[...]) * SCALE * sign_ref[...]


def unpack(packed_q, packed_kv, had, signs):
    groups, _, half, wide = packed_q.shape
    shape = lambda width: jax.ShapeDtypeStruct((2 * half, groups * width), jnp.float32)
    block = lambda width: pl.BlockSpec((half, width), lambda g, h: (h, g))
    return pl.pallas_call(
        unpack_kernel,
        out_shape=(shape(wide), shape(HEAD), shape(HEAD)),
        grid=(groups, 2),
        in_specs=[
            pl.BlockSpec((1, 1, half, wide), lambda g, h: (g, h, 0, 0)),
            pl.BlockSpec((1, 1, 2, half, HEAD), lambda g, h: (g, h, 0, 0, 0)),
            pl.BlockSpec((HEAD, HEAD), lambda g, h: (0, 0)),
            pl.BlockSpec((1, HEAD), lambda g, h: (0, 0)),
        ],
        out_specs=(block(wide), block(HEAD), block(HEAD)),
        compiler_params=pltpu.CompilerParams(vmem_limit_bytes=32 * 1024 * 1024),
        name="unpack",
    )(packed_q, packed_kv, had, signs)


def on_device(query, keys, values, attended, output_gradient, segments):
    tok = query.shape[1]
    half = tok // 2
    count = lax.axis_size("ctx")
    sections = lax.axis_size("section")
    had, signs = tables()
    seg = jnp.broadcast_to(segments[0].reshape(2, 1, half), (2, 8, half))
    packed_q, packed_kv = exchange_grads(
        count, sections, query[0], output_gradient[0], attended[0], keys[0], values[0],
        seg, had, signs,
    )
    out_q, out_k, out_v = unpack(packed_q, packed_kv, had, signs)
    return (out_q[None], out_k[None], out_v[None])


def solution(mesh):
    spec = P("section", "ctx", "head")
    return jax.shard_map(
        on_device,
        mesh=mesh,
        in_specs=(spec, spec, spec, spec, spec, P("section", "ctx")),
        out_specs=(spec, spec, spec),
        check_vma=False,
    )
```

time: 199 us -> 125 us (0.63)
  Pallas kernels: 72.1 us -> 119 us
  waiting for transfers between devices: 45.6 us -> 0 us
  blocking collectives: 40.9 us -> 0 us
  between operations: 14.2 us -> 0.67 us
  starting transfers between devices: 9.44 us -> 0 us
  local copies, waits for them, and re-layouts: 10 us -> 3.77 us
  other arithmetic: 5.31 us -> 1.34 us
    pallas_call x7 -> x2, Pallas kernels: 72.1 us -> 119 us  [the longest x1 116 us: exchange_grads(): pl.pallas_call(functools.partial(mega_kernel, count, groups, half, sectio...]
    ppermute x13 -> x0, waiting for transfers between devices: 45.6 us -> none  [shift(): return lax.ppermute(value, axis, pairs)]
    all_gather x1 -> x0, blocking collectives: 40.9 us -> none  [on_device(): seg_all = lax.all_gather(seg, 'ctx', axis=0, tiled=True)]
    ppermute x13 -> x0, starting transfers between devices: 9.41 us -> none  [shift(): return lax.ppermute(value, axis, pairs)]
    dynamic_slice x2 -> x0, local copies, waits for them, and re-layouts: 2.86 us -> none  [on_device(): part = lax.dynamic_slice(dkv, ((me + k) % count * tok, 0), (tok, 2 * HEAD))]
    reduce_sum x1 -> x0, other arithmetic: 2.03 us -> none  [on_device(): jnp.sum((last < seg[h * half]).astype(jnp.int32))]
  transfers between devices with their start and end apart: 14 -> 0, of which waited for: 5 -> 0; matrix products, arithmetic and copies ran while one was open for 6% -> 0% of each run, Pallas kernels for 20% -> 0%
where the time goes in v1:
time: 125 us
  Pallas kernels  119 us (95%)
  local copies, waits for them, and re-layouts  3.77 us (3%)
  other arithmetic  1.34 us (1%)
    pallas_call x1, Pallas kernels, exchange_grads(): pl.pallas_call(functools.partial(mega_kernel, count, groups, half, sectio...  116 us
    unnamed x9, local copies, waits for them, and re-layouts  3.15 us
    pallas_call x1, Pallas kernels, unpack(): pl.pallas_call(unpack_kernel, out_shape=(shape(wide), shape(HEAD), shape(...  3.11 us

profile of v1, /device:TPU:26, one launch (start us, length us, event | category | flops | bytes accessed | tf_op | source)
XLA Modules:
  0.0 124.8 jit_solution(7275715985522899418)
XLA Ops:
  0.6 0.5 broadcast.3
  1.1 1.3 %reduce.3 = s32[512]{0:T(512)S(1)} reduce(s32[1,512]{1,0:T(1,128)} %param.13, s32[]{:T(128)} %broadcast.3), dimensions={0}, to_apply=%param.13.reduce_sub_computation.3 | reduce | bytes 4100 | tf_op args[5]
  2.5 0.6 broadcast_in_dim.17.seg_ref
  3.1 0.0 copy-start.2
  3.1 0.0 copy-start.3
  3.1 115.9 %exchange_grads.1 = (bf16[2,2,256,1024]{3,2,1,0:T(8,128)(2,1)}, bf16[2,2,2,256,128]{4,3,2,1,0:T(8,128)(2,1)}) custom-call(bf16[512,2048]{1,0:T(8,128)(2,1)} %bitcast.9, bf16[512,2048]{1,0:T(8,128)(2,1)} %bitcast.10, bf16[512,2048]{1,0:T(8,128)(2,1)} %bitcast.11, bf16[512,256]{1,0:T(8,128)(2,1)} %bitcast.14, bf16[512,256]{1,0:T(8,128)(2,1)} %bitcast.15, ...), custom_call_target="tpu_custom_call" | custom-call | flops 24000000000 | bytes 16000000 | tf_op jit(solution)/shard_map/exchange_grads/pallas_call | solution.py:279
  119.0 0.0 copy-done.2
  119.0 0.0 copy-done.3
  119.0 0.0 copy-start
  119.0 1.6 %copy-done = bf16[2,2,256,1024]{3,2,1,0:T(8,128)(2,1)S(1)} copy-done((bf16[2,2,256,1024]{3,2,1,0:T(8,128)(2,1)S(1)}, bf16[2,2,256,1024]{3,2,1,0:T(8,128)(2,1)}, u32[]{:S(2)}) %copy-start) | copy-done | bytes 2097176
  120.6 0.0 copy-start.1
  120.6 1.0 copy-done.1
  121.6 3.1 %unpack.1 = (f32[512,2048]{1,0:T(8,128)}, f32[512,256]{1,0:T(8,128)}, f32[512,256]{1,0:T(8,128)}) custom-call(bf16[2,2,256,1024]{3,2,1,0:T(8,128)(2,1)S(1)} %copy-done, bf16[2,2,2,256,128]{4,3,2,1,0:T(8,128)(2,1)S(1)} %copy-done.1, bf16[128,128]{1,0:T(8,128)(2,1)S(1)} %copy-done.2, f32[1,128]{1,0:T(1,128)S(1)} %copy-done.3), custom_call_target="tpu_custom_call" | custom-call | tf_op jit(solution)/shard_map/unpack/pallas_call | solution.py:335
  (1 shorter events, 0.0 us)
Async XLA Ops:
  3.1 115.9 %copy-start.2 = (bf16[128,128]{1,0:T(8,128)(2,1)S(1)}, bf16[128,128]{1,0:T(8,128)(2,1)}, u32[]{:S(2)}) copy-start(bf16[128,128]{1,0:T(8,128)(2,1)} %constant.4.clone.had_ref) | copy-start | bytes 98308
  3.1 115.9 %copy-start.3 = (f32[1,128]{1,0:T(1,128)S(1)}, f32[1,128]{1,0:T(1,128)}, u32[]{:S(2)}) copy-start(f32[1,128]{1,0:T(1,128)} %constant.5.clone.sign_ref) | copy-start | bytes 1540
  119.0 1.6 %copy-start = (bf16[2,2,256,1024]{3,2,1,0:T(8,128)(2,1)S(1)}, bf16[2,2,256,1024]{3,2,1,0:T(8,128)(2,1)}, u32[]{:S(2)}) copy-start(bf16[2,2,256,1024]{3,2,1,0:T(8,128)(2,1)} %get-tuple-element.8.q_ref) | copy-start | bytes 6291460
  120.6 1.0 copy-start.1

commit v2 on v1

--- a/solution.py
+++ b/solution.py
@@ -38,12 +38,12 @@
 
 def mega_kernel(
     count, groups, half, sections,
-    q_ref, g_ref, a_ref, k_ref, v_ref, seg_ref, had_ref, sign_ref,
+    q_hbm, g_hbm, a_hbm, k_ref, v_ref, seg_ref, had_ref, sign_ref,
     rq_ref, rkv_ref,
-    kv_buf, seg_buf, dkv_out, part, own, q_pack, kv_pack,
+    q_ref, g_ref, a_ref, kv_buf, seg_buf, dkv_out, part, own, q_pack, kv_pack,
     s_ref, dk_acc, dv_acc, dq_acc, m_ref, l_ref, delta_ref,
     kv_send, kv_recv, seg_send, seg_recv, part_send, part_recv,
-    q_send, q_recv, back_send, back_recv,
+    q_send, q_recv, back_send, back_recv, load_sem,
 ):
     me = lax.axis_index("ctx")
     section = lax.axis_index("section")
@@ -90,6 +90,10 @@
             {"section": before},
         )
 
+    loads = [
+        pltpu.make_async_copy(src, dst, load_sem.at[i])
+        for i, (src, dst) in enumerate(((g_hbm, g_ref), (a_hbm, a_ref), (q_hbm, q_ref)))
+    ]
     barrier = pltpu.get_barrier_semaphore()
     for d in range(1, count):
         pl.semaphore_signal(
@@ -98,7 +102,10 @@
     pl.semaphore_signal(
         barrier, inc=1, device_id={"section": after}, device_id_type=pl.DeviceIdType.MESH
     )
-    seg_buf[me] = seg_ref[...]
+    for load in loads:
+        load.start()
+    for h in range(2):
+        seg_buf[me, h] = jnp.broadcast_to(seg_ref[:, h * half:(h + 1) * half], (8, half))
     for g in range(groups):
         for h in range(2):
             rows = slice(h * half, (h + 1) * half)
@@ -109,7 +116,8 @@
 
     for d in range(1, count):
         seg_copy(me, d, peer(d)).start()
-    for g in range(groups):
+
+    def send_keys(g):
         for d in range(1, count):
             kv_copy(g, 0, me, d, peer(d)).start()
         for d in range(1, count):
@@ -117,12 +125,33 @@
             def _():
                 kv_copy(g, 1, me, d, peer(d)).start()
 
+    send_keys(0)
+    for load in loads:
+        load.wait()
     for d in range(1, count):
         seg_copy(peer(d), d, peer(d)).wait_recv()
 
     def place(j):
         low = j < count
         return jnp.where(low, j, 2 * count - 1 - j), jnp.where(low, 0, 1)
+
+    def finish(g):
+        for h in range(2):
+            for d in range(1, count):
+                source = peer(d)
+
+                def add():
+                    part_arrival(g, h, source).wait_recv()
+                    own[g, h] += part[g, source, h].astype(jnp.float32)
+
+                if h == 0:
+                    add()
+                else:
+                    pl.when(source < me)(add)
+            for i in range(2):
+                flipped = (own[g, h, i] * sign_ref[...]).astype(jnp.bfloat16)
+                kv_pack[g, h, i] = (dot(flipped, had_ref[...]) * SCALE).astype(jnp.bfloat16)
+        back_copy(g).start()
 
     def do_group(g):
         base = g * wide
@@ -132,7 +161,7 @@
         def do_half(h, _):
             block = jnp.where(h == 0, me, 2 * count - 1 - me)
             rows = pl.ds(pl.multiple_of(h * half, half), half)
-            segq = seg_ref[h, 0:1, :]
+            segq = seg_buf[me, h, 0:1, :]
             qpos = block * half + lax.broadcasted_iota(jnp.int32, (1, half), 1)
             m_ref[...] = jnp.full_like(m_ref, NEG)
             l_ref[...] = jnp.zeros_like(l_ref)
@@ -173,6 +202,8 @@
                 return 0
 
             lax.fori_loop(0, block + 1, first, 0)
+            if g + 1 < groups:
+                pl.when(h == 1)(lambda: send_keys(g + 1))
             for r in range(REP):
                 m = m_ref[r]
                 top = jnp.max(m, axis=0, keepdims=True)
@@ -198,6 +229,13 @@
                     dq_acc[r] += dot(kt, ds)
                 dk_acc[slab, kh] = dk
                 dv_acc[slab, kh] = dv
+
+                @pl.when((h == 1) & (slab != me))
+                def _():
+                    dkv_out[g, slab, kh, 0] = (dk * SCALE).astype(jnp.bfloat16)
+                    dkv_out[g, slab, kh, 1] = dv.astype(jnp.bfloat16)
+                    part_copy(g, kh, lax.rem(slab - me + count, count), slab).start()
+
                 return 0
 
             lax.fori_loop(0, block + 1, second, 0)
@@ -206,47 +244,18 @@
                 turned = dot(dq.astype(jnp.bfloat16), had_ref[...]) * SCALE
                 q_pack[g, h, :, r * HEAD:(r + 1) * HEAD] = turned.astype(jnp.bfloat16)
             q_copy(g, h).start()
+            if g > 0:
+                pl.when(h == 0)(lambda: finish(g - 1))
             return 0
 
         lax.fori_loop(0, 2, do_half, 0)
         for h in range(2):
             own[g, h, 0] = dk_acc[me, h] * SCALE
             own[g, h, 1] = dv_acc[me, h]
-            for d in range(1, count):
-                to = peer(d)
-
-                def send():
-                    dkv_out[g, to, h, 0] = (dk_acc[to, h] * SCALE).astype(jnp.bfloat16)
-                    dkv_out[g, to, h, 1] = dv_acc[to, h].astype(jnp.bfloat16)
-                    part_copy(g, h, d, to).start()
-
-                if h == 0:
-                    send()
-                else:
-                    pl.when(to > me)(send)
-
-    def finish(g):
-        for h in range(2):
-            for d in range(1, count):
-                source = peer(d)
-
-                def add():
-                    part_arrival(g, h, source).wait_recv()
-                    own[g, h] += part[g, source, h].astype(jnp.float32)
-
-                if h == 0:
-                    add()
-                else:
-                    pl.when(source < me)(add)
-            for i in range(2):
-                flipped = (own[g, h, i] * sign_ref[...]).astype(jnp.bfloat16)
-                kv_pack[g, h, i] = (dot(flipped, had_ref[...]) * SCALE).astype(jnp.bfloat16)
-        back_copy(g).start()
 
     for g in range(groups):
         do_group(g)
-    for g in range(groups):
-        finish(g)
+    finish(groups - 1)
 
     for d in range(1, count):
         seg_copy(me, d, peer(d)).wait_send()
@@ -282,9 +291,12 @@
             jax.ShapeDtypeStruct((groups, 2, half, wide), low),
             jax.ShapeDtypeStruct((groups, 2, 2, half, HEAD), low),
         ),
-        in_specs=[vmem] * 8,
+        in_specs=[anywhere] * 3 + [vmem] * 5,
         out_specs=(anywhere, anywhere),
         scratch_shapes=[
+            pltpu.VMEM((tok, columns), low),
+            pltpu.VMEM((tok, columns), low),
+            pltpu.VMEM((tok, columns), low),
             pltpu.VMEM((groups, count, 2, 2, half, HEAD), low),
             pltpu.VMEM((count, 2, 8, half), jnp.int32),
             pltpu.VMEM((groups, count, 2, 2, half, HEAD), low),
@@ -309,6 +321,7 @@
             dma((groups, 2)),
             dma((groups,)),
             dma((groups,)),
+            dma((3,)),
         ],
         compiler_params=pltpu.CompilerParams(
             vmem_limit_bytes=60 * 1024 * 1024, collective_id=0, has_side_effects=True
@@ -343,21 +356,18 @@
             pl.BlockSpec((1, HEAD), lambda g, h: (0, 0)),
         ],
         out_specs=(block(wide), block(HEAD), block(HEAD)),
-        compiler_params=pltpu.CompilerParams(vmem_limit_bytes=32 * 1024 * 1024),
+        compiler_params=pltpu.CompilerParams(vmem_limit_bytes=60 * 1024 * 1024),
         name="unpack",
     )(packed_q, packed_kv, had, signs)
 
 
 def on_device(query, keys, values, attended, output_gradient, segments):
-    tok = query.shape[1]
-    half = tok // 2
     count = lax.axis_size("ctx")
     sections = lax.axis_size("section")
     had, signs = tables()
-    seg = jnp.broadcast_to(segments[0].reshape(2, 1, half), (2, 8, half))
     packed_q, packed_kv = exchange_grads(
         count, sections, query[0], output_gradient[0], attended[0], keys[0], values[0],
-        seg, had, signs,
+        segments, had, signs,
     )
     out_q, out_k, out_v = unpack(packed_q, packed_kv, had, signs)
     return (out_q[None], out_k[None], out_v[None])

time: 125 us -> 107 us (0.86); the launches traced: 125 us -> 105 us
  Pallas kernels: 119 us -> 105 us
  local copies, waits for them, and re-layouts: 3.77 us -> 0 us
  other arithmetic: 1.34 us -> 0 us
    pallas_call x1, Pallas kernels: 116 us -> 99.8 us  [exchange_grads(): pl.pallas_call(functools.partial(mega_kernel, count, groups, half, sectio...]
    unnamed x9 -> x0, local copies, waits for them, and re-layouts: 3.15 us -> none
    pallas_call x1, Pallas kernels: 3.11 us -> 4.95 us  [unpack(): pl.pallas_call(unpack_kernel, out_shape=(shape(wide), shape(HEAD), shape(...]
    unnamed x1 -> x0, other arithmetic: 1.34 us -> none
where the time goes in v2:
time: 107 us; the launch traced here: 105 us
  Pallas kernels  105 us (98%)
    pallas_call x1, Pallas kernels, exchange_grads(): pl.pallas_call(functools.partial(mega_kernel, count, groups, half, sectio...  99.8 us
    pallas_call x1, Pallas kernels, unpack(): pl.pallas_call(unpack_kernel, out_shape=(shape(wide), shape(HEAD), shape(...  4.95 us

profile of v2, /device:TPU:26, one launch (start us, length us, event | category | flops | bytes accessed | tf_op | source)
XLA Modules:
  0.0 105.3 jit_solution(16609518400002679496)
XLA Ops:
  0.6 99.8 %exchange_grads.1 = (bf16[2,2,256,1024]{3,2,1,0:T(8,128)(2,1)}, bf16[2,2,2,256,128]{4,3,2,1,0:T(8,128)(2,1)}) custom-call(bf16[512,2048]{1,0:T(8,128)(2,1)} %bitcast.9, bf16[512,2048]{1,0:T(8,128)(2,1)} %bitcast.10, bf16[512,2048]{1,0:T(8,128)(2,1)} %bitcast.11, bf16[512,256]{1,0:T(8,128)(2,1)} %bitcast.14, bf16[512,256]{1,0:T(8,128)(2,1)} %bitcast.15, ...), custom_call_target="tpu_custom_call" | custom-call | flops 24000000000 | bytes 16000000 | tf_op jit(solution)/shard_map/exchange_grads/pallas_call | solution.py:288
  100.4 4.9 %unpack.1 = (f32[512,2048]{1,0:T(8,128)}, f32[512,256]{1,0:T(8,128)}, f32[512,256]{1,0:T(8,128)}) custom-call(bf16[2,2,256,1024]{3,2,1,0:T(8,128)(2,1)} %get-tuple-element.8.q_ref, bf16[2,2,2,256,128]{4,3,2,1,0:T(8,128)(2,1)} %get-tuple-element.9.kv_ref, bf16[128,128]{1,0:T(8,128)(2,1)} %constant.4.clone.had_ref, f32[1,128]{1,0:T(1,128)} %constant.5.clone.sign_ref), custom_call_target="tpu_custom_call" | custom-call | tf_op jit(solution)/shard_map/unpack/pallas_call | solution.py:348

commit v3 on v2

--- a/solution.py
+++ b/solution.py
@@ -41,7 +41,7 @@
     q_hbm, g_hbm, a_hbm, k_ref, v_ref, seg_ref, had_ref, sign_ref,
     rq_ref, rkv_ref,
     q_ref, g_ref, a_ref, kv_buf, seg_buf, dkv_out, part, own, q_pack, kv_pack,
-    s_ref, dk_acc, dv_acc, dq_acc, m_ref, l_ref, delta_ref,
+    s_ref, dk_acc, dv_acc, dq_acc, m_ref, l_ref, delta_ref, top_ref,
     kv_send, kv_recv, seg_send, seg_recv, part_send, part_recv,
     q_send, q_recv, back_send, back_recv, load_sem,
 ):
@@ -173,7 +173,8 @@
                 )
                 delta_ref[r] = jnp.sum(prod.T, axis=0, keepdims=True)
 
-            def first(j, _):
+            def first(i, _):
+                j = jnp.where(h == 0, block - i, i)
                 slab, kh = place(j)
                 fresh = jnp.where(h == 0, 0, me + 1)
 
@@ -191,14 +192,14 @@
                 for r in range(REP):
                     qr = q_ref[rows, base + r * HEAD:base + (r + 1) * HEAD]
                     t = dot(kj, qr, NT) * (SCALE * LOG2E) + bias
-                    s_ref[r, at, :] = t
                     t = t.reshape(half // 8, 8, half)
                     m = m_ref[r]
                     new = jnp.maximum(m, jnp.max(t, axis=0))
                     m_ref[r] = new
-                    l_ref[r] = l_ref[r] * jnp.exp2(m - new) + jnp.sum(
-                        jnp.exp2(t - new[None]), axis=0
-                    )
+                    top_ref[r, j] = new
+                    e = jnp.exp2(t - new[None])
+                    s_ref[r, at, :] = e.reshape(half, half)
+                    l_ref[r] = l_ref[r] * jnp.exp2(m - new) + jnp.sum(e, axis=0)
                 return 0
 
             lax.fori_loop(0, block + 1, first, 0)
@@ -221,7 +222,9 @@
                     cols = slice(base + r * HEAD, base + (r + 1) * HEAD)
                     qr = q_ref[rows, cols]
                     gr = g_ref[rows, cols]
-                    p = jnp.exp2(s_ref[r, at, :] - m_ref[r, 0:1, :])
+                    f = jnp.exp2(top_ref[r, j] - m_ref[r, 0:1, :])
+                    e = s_ref[r, at, :].reshape(half // 8, 8, half)
+                    p = (e * f[None]).reshape(half, half)
                     dp = dot(vj, gr, NT)
                     ds = (p * (dp - delta_ref[r])).astype(jnp.bfloat16)
                     dv = dv + dot(p.astype(jnp.bfloat16), gr)
@@ -311,6 +314,7 @@
             pltpu.VMEM((REP, 8, half), full),
             pltpu.VMEM((REP, 8, half), full),
             pltpu.VMEM((REP, 1, half), full),
+            pltpu.VMEM((REP, 2 * count, 8, half), full),
             dma((groups, 2, count)),
             dma((groups, 2, count)),
             dma((count,)),

time: 107 us -> 108 us (level)
  no operation moved by 1% of the time
where the time goes in v3:
time: 108 us; the launch traced here: 106 us
  Pallas kernels  105 us (97%)
    pallas_call x1, Pallas kernels, exchange_grads(): pl.pallas_call(functools.partial(mega_kernel, count, groups, half, sectio...  100 us
    pallas_call x1, Pallas kernels, unpack(): pl.pallas_call(unpack_kernel, out_shape=(shape(wide), shape(HEAD), shape(...  4.96 us

profile of v3, /device:TPU:26, one launch (start us, length us, event | category | flops | bytes accessed | tf_op | source)
XLA Modules:
  0.0 105.6 jit_solution(507691649121235711)
XLA Ops:
  0.6 100.0 %exchange_grads.1 = (bf16[2,2,256,1024]{3,2,1,0:T(8,128)(2,1)}, bf16[2,2,2,256,128]{4,3,2,1,0:T(8,128)(2,1)}) custom-call(bf16[512,2048]{1,0:T(8,128)(2,1)} %bitcast.9, bf16[512,2048]{1,0:T(8,128)(2,1)} %bitcast.10, bf16[512,2048]{1,0:T(8,128)(2,1)} %bitcast.11, bf16[512,256]{1,0:T(8,128)(2,1)} %bitcast.14, bf16[512,256]{1,0:T(8,128)(2,1)} %bitcast.15, ...), custom_call_target="tpu_custom_call" | custom-call | flops 24000000000 | bytes 16000000 | tf_op jit(solution)/shard_map/exchange_grads/pallas_call | solution.py:291
  100.6 5.0 %unpack.1 = (f32[512,2048]{1,0:T(8,128)}, f32[512,256]{1,0:T(8,128)}, f32[512,256]{1,0:T(8,128)}) custom-call(bf16[2,2,256,1024]{3,2,1,0:T(8,128)(2,1)} %get-tuple-element.8.q_ref, bf16[2,2,2,256,128]{4,3,2,1,0:T(8,128)(2,1)} %get-tuple-element.9.kv_ref, bf16[128,128]{1,0:T(8,128)(2,1)} %constant.4.clone.had_ref, f32[1,128]{1,0:T(1,128)} %constant.5.clone.sign_ref), custom_call_target="tpu_custom_call" | custom-call | tf_op jit(solution)/shard_map/unpack/pallas_call | solution.py:352
